TPU v7x, 32 devices: a whole 2x2x4 slice. The times are simulated.
32 devices in a mesh: shot: 2 (over x), gx: 4 (over y, core), gy: 4 (over z).
Axes of the slice: x: 2, y: 2, z: 4, core: 2. Of those that a mesh axis runs over, the one named last changes fastest.
Arguments:
- forward: bfloat16 [2, 2, 9, 16, 512, 512], P('shot', None, None, None, 'gx', 'gy'), may hold values from -6 to 6
- adjoint: bfloat16 [2, 2, 9, 16, 512, 512], P('shot', None, None, None, 'gx', 'gy'), may hold values from -6 to 6
- snap_times: int32 [2, 2], P('shot'), may hold values from 1 to 32, as said below
- sources: int32 [2, 2], P('shot'), may hold values from 0 to 511
- aperture: int32 [2, 4, 4], P('shot', 'gx', 'gy'), may hold values 0 or 1
Outputs:
- smoothed: float32 [3, 16, 512, 512], P(None, 'shot', 'gx', 'gy')
Inputs may be any that keep to these rules, and one draw needn't show every extreme that they name: `snap_times`: each shot's times rise strictly, the first and every step from one to the next being 1 to 16; some shot takes steps of 16 throughout.
All inputs are finite; a program needn't handle non-finite values. No bound on the sum of `aperture` on one device may be relied on, other than what follows from the above.
Results may differ from a plain program's by a relative error of at most 0.0003.
Values sent between devices are 32-bit elements; how exact they have to be, the bound alone decides.
A program may use at most 64 MiB of HBM per device.

v0:
```python
import jax
import jax.numpy as jnp
from jax import lax
from jax.sharding import PartitionSpec as P

RADIUS = 16
MUTE = 32


spread_x = 0.5
spread_y = 0.375


def extended(cells, sides, width):
    for axis, dim in sides:
        count = lax.axis_size(axis)
        ends = count - 1
        head = lax.slice_in_dim(cells, 0, width, axis=dim)
        tail = lax.slice_in_dim(cells, cells.shape[dim] - width, cells.shape[dim], axis=dim)
        cells = jnp.concatenate(
            [
                lax.ppermute(tail, axis, [(i, (i + 1) % count) for i in range(ends)]),
                cells,
                lax.ppermute(head, axis, [((i + 1) % count, i) for i in range(ends)]),
            ],
            axis=dim,
        )
    return cells


def band_matrix(count, sigma):
    row_ids = lax.iota(jnp.int32, count)[:, None]
    col_ids = lax.iota(jnp.int32, count + 2 * RADIUS)[None, :]
    offset = col_ids - row_ids - RADIUS
    offset_real = offset.astype(jnp.float32)
    tap_list = jnp.arange(-RADIUS, RADIUS + 1).astype(jnp.float32)
    kernel_sum = jnp.sum(jnp.exp(-tap_list * tap_list / (2.0 * sigma * sigma)))
    values = jnp.exp(-offset_real * offset_real / (2.0 * sigma * sigma)) / kernel_sum
    return jnp.where(jnp.abs(offset) <= RADIUS, values, 0.0)


def on_device(forward, adjoint, snap_times, sources, aperture):
    steps_here = snap_times[0]
    earlier = jnp.concatenate([jnp.zeros((1,), jnp.int32), steps_here[:-1]])
    weights = (steps_here - earlier).astype(jnp.float32) / 8.0
    gradient = None
    for which in range(forward.shape[1]):
        forward_now = forward[0, which]
        adjoint_now = adjoint[0, which]

        def product(comp):
            return forward_now[comp].astype(jnp.float32) * adjoint_now[comp].astype(jnp.float32)

        density_term = product(0) + product(1) + product(2)
        trace_fwd = (
            forward_now[3].astype(jnp.float32)
            + forward_now[4].astype(jnp.float32)
            + forward_now[5].astype(jnp.float32)
        )
        trace_adj = (
            adjoint_now[3].astype(jnp.float32)
            + adjoint_now[4].astype(jnp.float32)
            + adjoint_now[5].astype(jnp.float32)
        )
        lame_term = trace_fwd * trace_adj
        shear_term = 2.0 * (
            product(3) + product(4) + product(5) + 2.0 * (product(6) + product(7) + product(8))
        )
        stacked = jnp.stack([lame_term, shear_term, density_term]) * -weights[which]
        gradient = stacked if gradient is None else gradient + stacked
    width_x = forward.shape[4]
    width_y = forward.shape[5]
    x_cells = lax.axis_index("gx") * width_x + lax.iota(jnp.int32, width_x)
    y_cells = lax.axis_index("gy") * width_y + lax.iota(jnp.int32, width_y)
    delta_x = (x_cells - sources[0, 0]).astype(jnp.float32)
    delta_y = (y_cells - sources[0, 1]).astype(jnp.float32)
    distance = (delta_x * delta_x)[:, None] + (delta_y * delta_y)[None, :]
    taper = (1.0 - jnp.exp(-distance / (2.0 * MUTE * MUTE))) * aperture[0, 0, 0].astype(jnp.float32)
    tapered = gradient * taper
    summed = lax.psum_scatter(tapered, "shot", scatter_dimension=1, tiled=True)
    across_x = band_matrix(width_x, spread_x * RADIUS)
    across_y = band_matrix(width_y, spread_y * RADIUS)
    wide_x = extended(summed, (("gx", 2),), RADIUS)
    smooth_x = jnp.einsum("ij,pljy->pliy", across_x, wide_x, precision=lax.Precision.HIGHEST)
    wide_y = extended(smooth_x, (("gy", 3),), RADIUS)
    return jnp.einsum("zy,pliy->pliz", across_y, wide_y, precision=lax.Precision.HIGHEST)


def solution(mesh):
    in_specs = (
        P("shot", None, None, None, "gx", "gy"),
        P("shot", None, None, None, "gx", "gy"),
        P("shot", None),
        P("shot", None),
        P("shot", "gx", "gy"),
    )
    out_specs = P(None, "shot", "gx", "gy")
    return jax.shard_map(
        on_device, mesh=mesh, in_specs=in_specs, out_specs=out_specs, check_vma=False
    )
```

profile of v0, /device:TPU:1, one launch (start us, length us, event | category | flops | bytes accessed | tf_op | source)
XLA Modules:
  0.0 119.4 jit_solution(4423931512987553202)
XLA Ops:
  6.5 0.0 reduce-scatter.5.cloned.1.call-start
  6.5 0.0 copy-start
  6.5 4.7 %fusion.25 = (f32[1,16,128,128]{3,2,1,0:T(8,128)S(1)}, f32[1,16,128,128]{3,2,1,0:T(8,128)S(1)}, f32[1,16,128,128]{3,2,1,0:T(8,128)S(1)}) fusion(bf16[1,2,9,16,128,128]{5,4,3,2,1,0:T(8,128)(2,1)} %param.6, bf16[1,2,9,16,128,128]{5,4,3,2,1,0:T(8,128)(2,1)} %param.5), kind=kLoop, calls=%fused_computation.40 | loop fusion | flops 8650752 | bytes 12582912 | tf_op jit(solution)/shard_map/mul | solution.py:65
  11.2 1.8 %copy-done = bf16[1,2,9,16,128,128]{5,4,3,2,1,0:T(8,128)(2,1)S(1)} copy-done((bf16[1,2,9,16,128,128]{5,4,3,2,1,0:T(8,128)(2,1)S(1)}, bf16[1,2,9,16,128,128]{5,4,3,2,1,0:T(8,128)(2,1)}, u32[]{:S(2)}) %copy-start) | copy-done | bytes 9437208
  13.0 4.2 %fusion.30 = (f32[1,16,128,128]{3,2,1,0:T(8,128)}, f32[1,16,128,128]{3,2,1,0:T(8,128)}) fusion(bf16[1,2,9,16,128,128]{5,4,3,2,1,0:T(8,128)(2,1)S(1)} %copy-done, bf16[1,2,9,16,128,128]{5,4,3,2,1,0:T(8,128)(2,1)} %param.5), kind=kLoop, calls=%fused_computation.45 | loop fusion | flops 9437184 | bytes 11534336 | tf_op jit(solution)/shard_map/mul | solution.py:66
  17.1 0.0 copy-start.1
  17.1 0.0 copy-start.2
  17.2 4.0 %fusion.23 = f32[1,16,128,128]{3,2,1,0:T(8,128)} fusion(bf16[1,2,9,16,128,128]{5,4,3,2,1,0:T(8,128)(2,1)S(1)} %copy-done, bf16[1,2,9,16,128,128]{5,4,3,2,1,0:T(8,128)(2,1)} %param.5), kind=kLoop, calls=%fused_computation.38 | loop fusion | flops 6553600 | bytes 7340032 | tf_op jit(solution)/shard_map/mul | solution.py:66
  21.1 0.0 copy-done.1
  21.1 0.6 fusion.66
  22.4 0.0 copy-done.2
  22.4 0.1 fusion.52
  22.5 0.6 fusion.65
  24.3 1.3 %convert_multiply_fusion.6 = (f32[128]{0:T(128)S(1)}, f32[128]{0:T(128)S(1)}) fusion(s32[]{:T(128)} %bitcast.11, s32[]{:T(128)S(6)} %mul.358, s32[]{:T(128)} %bitcast.10, s32[]{:T(128)S(6)} %mul.356), kind=kLoop, calls=%fused_computation.78 | loop fusion | flops 1024 | bytes 1040 | tf_op jit(solution)/shard_map/mul | solution.py:77
  25.6 0.1 subtract_multiply_fusion
  25.7 2.5 %fusion.1 = f32[3,16,128,128]{3,2,1,0:T(8,128)S(1)} fusion(f32[1,16,128,128]{3,2,1,0:T(8,128)S(1)} %get-tuple-element.6, f32[1,16,128,128]{3,2,1,0:T(8,128)} %fusion.23, f32[1,16,128,128]{3,2,1,0:T(8,128)S(1)} %get-tuple-element.7, f32[1,16,128,128]{3,2,1,0:T(8,128)} %get-tuple-element.9, f32[1,16,128,128]{3,2,1,0:T(8,128)} %get-tuple-element.8, ...), kind=kLoop, calls=%fused_computation.3 | loop fusion | flops 6291456 | bytes 9502728 | tf_op jit(solution)/shard_map/mul | solution.py:79
  28.3 0.3 copy.8
  28.6 3.5 %copy.14 = f32[2,8,384,128]{3,1,2,0:T(8,128)} copy(f32[2,8,384,128]{3,2,1,0:T(8,128)S(1)} %bitcast.49) | data formatting | bytes 6291456
  32.1 0.0 reduce-scatter.5.cloned.1.call-update
  32.1 45.6 %reduce-scatter.5.cloned.1.call-done = f32[8,49152]{1,0:T(8,128)} async-done(((f32[16,49152]{1,0:T(8,128)}), f32[8,49152]{1,0:T(8,128)}) %reduce-scatter.5.cloned.1.call-update) | async-done | bytes 1572880
  77.7 1.7 %copy.9 = f32[3,8,128,128]{3,2,1,0:T(8,128)S(1)} copy(f32[3,8,128,128]{3,1,2,0:T(8,128)} %bitcast.50) | data formatting | bytes 3145728
  79.4 3.7 %collective-permute-start = (f32[3,8,16,128]{3,2,1,0:T(8,128)S(1)}, f32[3,8,16,128]{3,2,1,0:T(8,128)S(1)}, u32[]{:S(2)}, u32[]{:S(2)}) collective-permute-start(f32[3,8,16,128]{3,2,1,0:T(8,128)S(1)} %get-tuple-element.12), channel_id=1, source_target_pairs={{0,4},{4,8},{8,12},{1,5},{5,9},{9,13},{2,6},{6,10},{10,14},{3,7},{... | collective-permute-start | bytes 589832 | tf_op jit(solution)/shard_map/ppermute | solution.py:22
  83.1 1.9 %collective-permute-start.1 = (f32[3,8,16,128]{3,2,1,0:T(8,128)S(1)}, f32[3,8,16,128]{3,2,1,0:T(8,128)S(1)}, u32[]{:S(2)}, u32[]{:S(2)}) collective-permute-start(f32[3,8,16,128]{3,2,1,0:T(8,128)S(1)} %get-tuple-element.13), channel_id=1, source_target_pairs={{4,0},{8,4},{12,8},{5,1},{9,5},{13,9},{6,2},{10,6},{14,10},{7,3},{... | collective-permute-start | bytes 589832 | tf_op jit(solution)/shard_map/ppermute | solution.py:24
  85.0 0.6 exponential_reduce_fusion.1
  85.6 0.0 collective-permute-done
  85.7 4.4 %collective-permute-done.1 = f32[3,8,16,128]{3,2,1,0:T(8,128)S(1)} collective-permute-done((f32[3,8,16,128]{3,2,1,0:T(8,128)S(1)}, f32[3,8,16,128]{3,2,1,0:T(8,128)S(1)}, u32[]{:S(2)}, u32[]{:S(2)}) %collective-permute-start.1) | collective-permute-done | bytes 196640 | tf_op jit(solution)/shard_map/ppermute | solution.py:24
  90.1 5.9 %fusion.14 = f32[3,8,128,128]{2,3,1,0:T(8,128)S(1)} fusion(f32[3,8,16,128]{3,2,1,0:T(8,128)S(1)} %collective-permute-done.1, f32[3,8,128,128]{3,2,1,0:T(8,128)S(1)} %copy.9, f32[3,8,16,128]{3,2,1,0:T(8,128)S(1)} %collective-permute-done, f32[]{:T(128)} %exponential_reduce_fusion.1), kind=kOutput, calls=%fused_computation.17 | convolution fusion | flops 756162560 | bytes 3538948 | tf_op jit(solution)/shard_map/ij,pljy->pliy/dot_general | solution.py:84
  96.0 3.1 %collective-permute-start.2 = (f32[3,8,128,16]{2,3,1,0:T(8,128)S(1)}, f32[3,8,128,16]{2,3,1,0:T(8,128)S(1)}, u32[]{:S(2)}, u32[]{:S(2)}) collective-permute-start(f32[3,8,128,16]{2,3,1,0:T(8,128)S(1)} %get-tuple-element.10), channel_id=1, source_target_pairs={{0,1},{1,2},{2,3},{4,5},{5,6},{6,7},{8,9},{9,10},{10,11},{12,13},{... | collective-permute-start | bytes 589832 | tf_op jit(solution)/shard_map/ppermute | solution.py:22
  99.2 1.5 %collective-permute-start.3 = (f32[3,8,128,16]{2,3,1,0:T(8,128)S(1)}, f32[3,8,128,16]{2,3,1,0:T(8,128)S(1)}, u32[]{:S(2)}, u32[]{:S(2)}) collective-permute-start(f32[3,8,128,16]{2,3,1,0:T(8,128)S(1)} %get-tuple-element.11), channel_id=1, source_target_pairs={{1,0},{2,1},{3,2},{5,4},{6,5},{7,6},{9,8},{10,9},{11,10},{13,12},{... | collective-permute-start | bytes 589832 | tf_op jit(solution)/shard_map/ppermute | solution.py:24
  100.6 0.7 exponential_reduce_fusion
  101.3 0.4 collective-permute-done.2
  101.8 3.8 %collective-permute-done.3 = f32[3,8,128,16]{2,3,1,0:T(8,128)S(1)} collective-permute-done((f32[3,8,128,16]{2,3,1,0:T(8,128)S(1)}, f32[3,8,128,16]{2,3,1,0:T(8,128)S(1)}, u32[]{:S(2)}, u32[]{:S(2)}) %collective-permute-start.3) | collective-permute-done | bytes 196640 | tf_op jit(solution)/shard_map/ppermute | solution.py:24
  105.6 7.0 %fusion.8 = f32[3,8,128,128]{3,2,1,0:T(8,128)} fusion(f32[3,8,128,16]{2,3,1,0:T(8,128)S(1)} %collective-permute-done.3, f32[3,8,128,128]{2,3,1,0:T(8,128)S(1)} %fusion.14, f32[3,8,128,16]{2,3,1,0:T(8,128)S(1)} %collective-permute-done.2, f32[]{:T(128)} %exponential_reduce_fusion), kind=kOutput, calls=%fused_computation.11 | convolution fusion | flops 756162560 | bytes 3538948 | tf_op jit(solution)/shard_map/zy,pliy->pliz/dot_general | solution.py:86
  (2 shorter events, 0.1 us)
Async XLA Ops:
  6.5 71.2 %reduce-scatter.5.cloned.1.call-start = ((), (), s32[]{:S(2)}) async-start(), calls=%async_computation.1 | async-start | bytes 4718592
  6.5 6.4 %copy-start = (bf16[1,2,9,16,128,128]{5,4,3,2,1,0:T(8,128)(2,1)S(1)}, bf16[1,2,9,16,128,128]{5,4,3,2,1,0:T(8,128)(2,1)}, u32[]{:S(2)}) copy-start(bf16[1,2,9,16,128,128]{5,4,3,2,1,0:T(8,128)(2,1)} %param.6) | copy-start | bytes 28311556
  17.1 4.0 %copy-start.1 = (s32[1,2]{1,0:T(1,128)S(1)}, s32[1,2]{1,0:T(1,128)}, u32[]{:S(2)}) copy-start(s32[1,2]{1,0:T(1,128)} %param.8) | copy-start | bytes 28
  17.1 5.3 %copy-start.2 = (s32[1,2]{1,0:T(1,128)S(1)}, s32[1,2]{1,0:T(1,128)}, u32[]{:S(2)}) copy-start(s32[1,2]{1,0:T(1,128)} %param.7) | copy-start | bytes 28
  79.4 6.3 %collective-permute-start = (f32[3,8,16,128]{3,2,1,0:T(8,128)S(1)}, f32[3,8,16,128]{3,2,1,0:T(8,128)S(1)}, u32[]{:S(2)}, u32[]{:S(2)}) collective-permute-start(f32[3,8,16,128]{3,2,1,0:T(8,128)S(1)} %get-tuple-element.12), channel_id=1, source_target_pairs={{0,4},{4,8},{8,12},{1,5},{5,9},{9,13},{2,6},{6,10},{10,14},{3,7},{... | collective-permute-start | bytes 589832 | tf_op jit(solution)/shard_map/ppermute | solution.py:22
  83.1 7.0 %collective-permute-start.1 = (f32[3,8,16,128]{3,2,1,0:T(8,128)S(1)}, f32[3,8,16,128]{3,2,1,0:T(8,128)S(1)}, u32[]{:S(2)}, u32[]{:S(2)}) collective-permute-start(f32[3,8,16,128]{3,2,1,0:T(8,128)S(1)} %get-tuple-element.13), channel_id=1, source_target_pairs={{4,0},{8,4},{12,8},{5,1},{9,5},{13,9},{6,2},{10,6},{14,10},{7,3},{... | collective-permute-start | bytes 589832 | tf_op jit(solution)/shard_map/ppermute | solution.py:24
  96.0 5.7 %collective-permute-start.2 = (f32[3,8,128,16]{2,3,1,0:T(8,128)S(1)}, f32[3,8,128,16]{2,3,1,0:T(8,128)S(1)}, u32[]{:S(2)}, u32[]{:S(2)}) collective-permute-start(f32[3,8,128,16]{2,3,1,0:T(8,128)S(1)} %get-tuple-element.10), channel_id=1, source_target_pairs={{0,1},{1,2},{2,3},{4,5},{5,6},{6,7},{8,9},{9,10},{10,11},{12,13},{... | collective-permute-start | bytes 589832 | tf_op jit(solution)/shard_map/ppermute | solution.py:22
  99.2 6.4 %collective-permute-start.3 = (f32[3,8,128,16]{2,3,1,0:T(8,128)S(1)}, f32[3,8,128,16]{2,3,1,0:T(8,128)S(1)}, u32[]{:S(2)}, u32[]{:S(2)}) collective-permute-start(f32[3,8,128,16]{2,3,1,0:T(8,128)S(1)} %get-tuple-element.11), channel_id=1, source_target_pairs={{1,0},{2,1},{3,2},{5,4},{6,5},{7,6},{9,8},{10,9},{11,10},{13,12},{... | collective-permute-start | bytes 589832 | tf_op jit(solution)/shard_map/ppermute | solution.py:24
Sparse Core Ops, SparseCore 0:
  32.2 45.4 reduce-scatter.4
where the time goes:
time: 120 us; the launch traced here: 119 us
  waiting for transfers between devices  54.3 us (45%)
  other arithmetic  18.1 us (15%)
  between operations  15.3 us (13%)
  matrix products  12.9 us (11%)
  starting transfers between devices  10.2 us (8%)
  local copies, waits for them, and re-layouts  8.6 us (7%)
    unnamed x2, waiting for transfers between devices  45.6 us
    ppermute x2, waiting for transfers between devices, extended(): lax.ppermute(head, axis, [((i + 1) % count, i) for i in range(ends)])  8.22 us
    mul x2, other arithmetic, on_device(): 2.0 * (product(3) + product(4) + product(5) + 2.0 * (product(6) + product...  8.12 us
    unnamed x9, local copies, waits for them, and re-layouts  7.28 us
    dot_general x1, matrix products, on_device(): jnp.einsum('zy,pliy->pliz', across_y, wide_y, precision=lax.Precision.HIG...  7 us
    ppermute x2, starting transfers between devices, extended(): lax.ppermute(tail, axis, [(i, (i + 1) % count) for i in range(ends)])  6.8 us
    dot_general x1, matrix products, on_device(): jnp.einsum('ij,pljy->pliy', across_x, wide_x, precision=lax.Precision.HIG...  5.91 us
    mul x1, other arithmetic, on_device(): lame_term = trace_fwd * trace_adj  4.65 us
  transfers between devices with their start and end apart: 5, of which 4 were waited for; matrix products, arithmetic and copies ran while one was open for 1% of the time, Pallas kernels for 0%

commit v1 on v0

v1 whole, which is shorter than its diff:
```python
import functools

import jax
import jax.numpy as jnp
import numpy as np
from jax import lax
from jax.experimental import pallas as pl
from jax.experimental.pallas import tpu as pltpu
from jax.sharding import PartitionSpec as P

RADIUS = 16
MUTE = 32
SIGMA_X = 0.5 * RADIUS
SIGMA_Y = 0.375 * RADIUS
ROWS = 16


def band_parts(count, sigma):
    taps = np.arange(-RADIUS, RADIUS + 1).astype(np.float64)
    norm = np.exp(-taps * taps / (2.0 * sigma * sigma)).sum()
    own = np.arange(count)
    cells = np.concatenate([own, np.arange(-RADIUS, 0), np.arange(count, count + RADIUS)])
    offset = (cells[:, None] - own[None, :]).astype(np.float64)
    values = np.exp(-offset * offset / (2.0 * sigma * sigma)) / norm
    values = np.where(np.abs(offset) <= RADIUS, values, 0.0).astype(np.float32)
    high = values.astype(jnp.bfloat16)
    low = (values - high.astype(np.float32)).astype(jnp.bfloat16)
    return np.concatenate([high, low], axis=1)


def kernel(
    n, ng, nh, raw,
    fwd, adj, times, sources, aperture, band_x, band_y,
    out,
    fbuf, abuf, taper, wx, wy, sm, recv,
    load_f, load_a, x_send, x_recv, gx_send, gx_recv, gy_send, gy_recv,
):
    me = lax.axis_index("shot")
    g = lax.axis_index("gx")
    h = lax.axis_index("gy")
    snaps = fwd.shape[1]
    levels = fwd.shape[3]
    width_x, width_y = fwd.shape[4], fwd.shape[5]
    here = levels // n
    peers = (n - 1) * here

    def load(q):
        level = lax.rem(me + q // here + 1, n) * here + lax.rem(q, here)
        return (
            pltpu.make_async_copy(fwd.at[0, :, :, level], fbuf.at[q], load_f.at[q]),
            pltpu.make_async_copy(adj.at[0, :, :, level], abuf.at[q], load_a.at[q]),
        )

    def start_load(q, c):
        for copy in load(q):
            copy.start()
        return c

    lax.fori_loop(0, levels, start_load, 0)

    barrier = pltpu.get_barrier_semaphore()
    for d in range(1, n):
        pl.semaphore_signal(barrier, inc=1, device_id={"shot": lax.rem(me + d, n)})
    greeted = jnp.int32(n - 1)
    for axis, at, count in (("gx", g, ng), ("gy", h, nh)):
        @pl.when(at > 0)
        def _():
            pl.semaphore_signal(barrier, inc=1, device_id={axis: at - 1})

        @pl.when(at < count - 1)
        def _():
            pl.semaphore_signal(barrier, inc=1, device_id={axis: at + 1})

        greeted = greeted + (at > 0).astype(jnp.int32) + (at < count - 1).astype(jnp.int32)

    for buf, at, count, width in ((wx, g, ng, width_x), (wy, h, nh, width_y)):
        for there, start in ((at > 0, width), (at < count - 1, width + RADIUS)):
            @pl.when(jnp.logical_not(there))
            def _():
                def clear(q, c):
                    buf[q, :, start:start + RADIUS, :] = jnp.zeros(
                        (3, RADIUS, buf.shape[3]), jnp.float32
                    )
                    return c

                lax.fori_loop(0, levels, clear, 0)

    x_at = g * width_x + lax.broadcasted_iota(jnp.int32, (width_x, width_y), 0)
    y_at = h * width_y + lax.broadcasted_iota(jnp.int32, (width_x, width_y), 1)
    dx = (x_at - sources[0, 0]).astype(jnp.float32)
    dy = (y_at - sources[0, 1]).astype(jnp.float32)
    taper[...] = (1.0 - jnp.exp(-(dx * dx + dy * dy) / (2.0 * MUTE * MUTE))) * aperture[
        0, 0, 0
    ].astype(jnp.float32)

    weights = []
    for k in range(snaps):
        step = times[0, k] - (times[0, k - 1] if k else 0)
        weights.append(step.astype(jnp.float32) * -0.125)

    def image(q):
        def rows_of(c, carry):
            rows = pl.ds(pl.multiple_of(c * ROWS, ROWS), ROWS)
            lame = shear = density = None
            for k in range(snaps):
                f = [fbuf[q, k, i, rows, :].astype(jnp.float32) for i in range(9)]
                a = [abuf[q, k, i, rows, :].astype(jnp.float32) for i in range(9)]
                w = weights[k]
                la = (f[3] + f[4] + f[5]) * (a[3] + a[4] + a[5]) * w
                sh = (
                    f[3] * a[3] + f[4] * a[4] + f[5] * a[5]
                    + 2.0 * (f[6] * a[6] + f[7] * a[7] + f[8] * a[8])
                ) * (2.0 * w)
                de = (f[0] * a[0] + f[1] * a[1] + f[2] * a[2]) * w
                if k == 0:
                    lame, shear, density = la, sh, de
                else:
                    lame, shear, density = lame + la, shear + sh, density + de
            t = taper[rows, :]
            wx[q, 0, rows, :] = lame * t
            wx[q, 1, rows, :] = shear * t
            wx[q, 2, rows, :] = density * t
            return carry

        lax.fori_loop(0, width_x // ROWS, rows_of, 0)

    def x_copy(src, q):
        d = q // here + 1
        return pltpu.make_async_remote_copy(
            src_ref=src,
            dst_ref=recv.at[q],
            send_sem=x_send.at[q],
            recv_sem=x_recv.at[q],
            device_id={"shot": lax.rem(me + d, n)},
        )

    def halo(axis, q):
        buf, at, count, width, send, recv_sem = (
            (wx, g, ng, width_x, gx_send, gx_recv)
            if axis == "gx"
            else (wy, h, nh, width_y, gy_send, gy_recv)
        )

        def copy(side):
            first = 0 if side == 0 else width - RADIUS
            lands = width + RADIUS if side == 0 else width
            other = lax.rem(at + (count - 1 if side == 0 else 1), count)
            return pltpu.make_async_remote_copy(
                src_ref=buf.at[q, :, pl.ds(first, RADIUS), :],
                dst_ref=buf.at[q, :, pl.ds(lands, RADIUS), :],
                send_sem=send.at[side, q],
                recv_sem=recv_sem.at[side, q],
                device_id={axis: other},
            )

        return copy, at > 0, at < count - 1

    def halo_start(axis, q):
        copy, left, right = halo(axis, q)
        pl.when(left)(lambda: copy(0).start())
        pl.when(right)(lambda: copy(1).start())

    def halo_arrived(axis, q):
        copy, left, right = halo(axis, q)
        pl.when(right)(lambda: copy(0).wait_recv())
        pl.when(left)(lambda: copy(1).wait_recv())

    def halo_sent(axis, q):
        copy, left, right = halo(axis, q)
        pl.when(left)(lambda: copy(0).wait_send())
        pl.when(right)(lambda: copy(1).wait_send())

    def smooth(cells, band):
        width = band.shape[1] // 2
        high = cells.astype(jnp.bfloat16)
        low = (cells - high.astype(jnp.float32)).astype(jnp.bfloat16)
        dims = (((0,), (0,)), ((), ()))
        both = lax.dot_general(high, band[...], dims, preferred_element_type=jnp.float32)
        rest = lax.dot_general(
            low, band[:, :width], dims, preferred_element_type=jnp.float32
        )
        return both[:, :width] + (both[:, width:] + rest)

    def along_x(q):
        halo_arrived("gx", q)
        for p in range(3):
            wy[q, p, 0:width_y, :] = smooth(wx[q, p], band_x)
        halo_start("gy", q)

    def is_raw(q):
        return lax.rem(q, here) < raw

    def make(q, c):
        for copy in load(q):
            copy.wait()
        image(q)

        @pl.when(q == 0)
        def _():
            pl.semaphore_wait(barrier, greeted)

        @pl.when(jnp.logical_and(is_raw(q), q < peers))
        def _():
            x_copy(wx.at[q, :, pl.ds(0, width_x), :], q).start()

        @pl.when(jnp.logical_not(is_raw(q)))
        def _():
            halo_start("gx", q)

        return c

    lax.fori_loop(0, levels, make, 0)

    def first_x(q, c):
        @pl.when(jnp.logical_not(is_raw(q)))
        def _():
            along_x(q)

        return c

    lax.fori_loop(0, levels, first_x, 0)

    def to_send(q, c):
        @pl.when(jnp.logical_not(is_raw(q)))
        def _():
            halo_arrived("gy", q)
            for p in range(3):
                sm[q, p] = smooth(wy[q, p], band_y)
            x_copy(sm.at[q], q).start()

        return c

    lax.fori_loop(0, peers, to_send, 0)

    def to_out(i, c):
        q = peers + i
        halo_arrived("gy", q)
        for p in range(3):
            out[p, i] = smooth(wy[q, p], band_y)
        return c

    lax.fori_loop(raw, here, to_out, 0)

    def sum_raw(i, c):
        for d in range(n - 1):
            q = d * here + i
            x_copy(wx.at[q, :, pl.ds(0, width_x), :], q).wait_recv()
        for p in range(3):
            total = wx[peers + i, p, 0:width_x, :]
            for d in range(n - 1):
                total = total + recv[d * here + i, p]
            wx[peers + i, p, 0:width_x, :] = total
        halo_start("gx", peers + i)
        return c

    lax.fori_loop(0, raw, sum_raw, 0)

    def raw_x(i, c):
        along_x(peers + i)
        return c

    lax.fori_loop(0, raw, raw_x, 0)
    lax.fori_loop(0, raw, to_out, 0)

    def add(i, c):
        for d in range(n - 1):
            q = d * here + i
            x_copy(sm.at[q], q).wait_recv()
        for p in range(3):
            total = out[p, i]
            for d in range(n - 1):
                total = total + recv[d * here + i, p]
            out[p, i] = total
        return c

    lax.fori_loop(raw, here, add, 0)

    def done(q, c):
        @pl.when(q < peers)
        def _():
            x_copy(sm.at[q], q).wait_send()

        @pl.when(jnp.logical_or(q >= peers, jnp.logical_not(is_raw(q))))
        def _():
            halo_sent("gx", q)
            halo_sent("gy", q)

        return c

    lax.fori_loop(0, levels, done, 0)


def on_device(n, ng, nh, forward, adjoint, snap_times, sources, aperture):
    snaps, comps, levels, width_x, width_y = forward.shape[1:]
    here = levels // n
    peers = (n - 1) * here
    raw = here // 2
    f32 = jnp.float32
    dma = pltpu.SemaphoreType.DMA
    smem = pl.BlockSpec(memory_space=pltpu.SMEM)
    vmem = pl.BlockSpec(memory_space=pltpu.VMEM)
    anywhere = pl.BlockSpec(memory_space=pl.ANY)
    return pl.pallas_call(
        functools.partial(kernel, n, ng, nh, raw),
        out_shape=jax.ShapeDtypeStruct((3, here, width_x, width_y), f32),
        in_specs=[anywhere, anywhere, smem, smem, smem, vmem, vmem],
        out_specs=vmem,
        scratch_shapes=[
            pltpu.VMEM((levels, snaps, comps, width_x, width_y), forward.dtype),
            pltpu.VMEM((levels, snaps, comps, width_x, width_y), adjoint.dtype),
            pltpu.VMEM((width_x, width_y), f32),
            pltpu.VMEM((levels, 3, width_x + 2 * RADIUS, width_y), f32),
            pltpu.VMEM((levels, 3, width_y + 2 * RADIUS, width_x), f32),
            pltpu.VMEM((peers, 3, width_x, width_y), f32),
            pltpu.VMEM((peers, 3, width_x, width_y), f32),
            dma((levels,)),
            dma((levels,)),
            dma((peers,)),
            dma((peers,)),
            dma((2, levels)),
            dma((2, levels)),
            dma((2, levels)),
            dma((2, levels)),
        ],
        compiler_params=pltpu.CompilerParams(
            collective_id=0, has_side_effects=True, vmem_limit_bytes=52 * 1024 * 1024
        ),
        cost_estimate=pl.CostEstimate(
            flops=2 * forward.size * 4,
            bytes_accessed=4 * forward.size + 12 * here * width_x * width_y,
            transcendentals=width_x * width_y,
        ),
    )(
        forward, adjoint, snap_times, sources, aperture,
        band_parts(width_x, SIGMA_X), band_parts(width_y, SIGMA_Y),
    )


def solution(mesh):
    in_specs = (
        P("shot", None, None, None, "gx", "gy"),
        P("shot", None, None, None, "gx", "gy"),
        P("shot", None),
        P("shot", None),
        P("shot", "gx", "gy"),
    )
    sizes = (mesh.shape["shot"], mesh.shape["gx"], mesh.shape["gy"])
    return jax.shard_map(
        functools.partial(on_device, *sizes),
        mesh=mesh,
        in_specs=in_specs,
        out_specs=P(None, "shot", "gx", "gy"),
        check_vma=False,
    )
```

time: 120 us -> 46.9 us (0.39)
  the two profiles are of different devices: /device:TPU:1 before, /device:TPU:0 now
where the time goes in v1:
time: 46.9 us; the launch traced here: 46.6 us
  Pallas kernels  41.8 us (89%)
  local copies, waits for them, and re-layouts  4.22 us (9%)
  between operations  0.67 us (1%)
    pallas_call x1, Pallas kernels, on_device(): pl.pallas_call(functools.partial(kernel, n, ng, nh, raw), out_shape=jax.S...  41.8 us
    unnamed x9, local copies, waits for them, and re-layouts  4.22 us

profile of v1, /device:TPU:0, one launch (start us, length us, event | category | flops | bytes accessed | tf_op | source)
XLA Modules:
  0.0 46.6 jit_solution(13140783222292246052)
XLA Ops:
  0.7 0.0 copy-start
  0.7 0.9 %copy-done = bf16[160,256]{1,0:T(8,128)(2,1)S(1)} copy-done((bf16[160,256]{1,0:T(8,128)(2,1)S(1)}, bf16[160,256]{1,0:T(8,128)(2,1)}, u32[]{:S(2)}) %copy-start) | copy-done | bytes 81944
  1.5 0.0 copy-start.1
  1.5 0.9 %copy-done.1 = bf16[160,256]{1,0:T(8,128)(2,1)S(1)} copy-done((bf16[160,256]{1,0:T(8,128)(2,1)S(1)}, bf16[160,256]{1,0:T(8,128)(2,1)}, u32[]{:S(2)}) %copy-start.1) | copy-done | bytes 81944
  2.4 0.0 copy-start.2
  2.4 0.7 %copy-done.2 = s32[1,2]{1,0:T(1,128)S(1)} copy-done((s32[1,2]{1,0:T(1,128)S(1)}, s32[1,2]{1,0:T(1,128)}, u32[]{:S(2)}) %copy-start.2) | copy-done | bytes 32
  3.1 0.0 copy-start.3
  3.1 0.7 %copy-done.3 = s32[1,2]{1,0:T(1,128)S(1)} copy-done((s32[1,2]{1,0:T(1,128)S(1)}, s32[1,2]{1,0:T(1,128)}, u32[]{:S(2)}) %copy-start.3) | copy-done | bytes 32
  3.7 41.8 %shard_map.73 = f32[3,8,128,128]{3,2,1,0:T(8,128)S(1)} custom-call(bf16[1,2,9,16,128,128]{5,4,3,2,1,0:T(8,128)(2,1)} %fwd.1, bf16[1,2,9,16,128,128]{5,4,3,2,1,0:T(8,128)(2,1)} %adj.1, s32[1,2]{1,0:T(1,128)S(1)} %copy-done.2, s32[1,2]{1,0:T(1,128)S(1)} %copy-done.3, s32[1,1,1]{2,1,0:T(1,128)S(6)} %copy.9.aperture, bf16[160,256]{1,0:T(8,128)(2,1)S(1)} %copy-done.1, ...), custom_call_target="tpu_custom_call" | custom-call | flops 37748736 | bytes 20447232 | tf_op jit(solution)/shard_map/pallas_call | solution.py:303
  45.5 1.1 %copy.10 = f32[3,8,128,128]{3,2,1,0:T(8,128)} copy(f32[3,8,128,128]{3,2,1,0:T(8,128)S(1)} %shard_map.73) | data formatting | bytes 3145728
Async XLA Ops:
  0.7 0.9 %copy-start = (bf16[160,256]{1,0:T(8,128)(2,1)S(1)}, bf16[160,256]{1,0:T(8,128)(2,1)}, u32[]{:S(2)}) copy-start(bf16[160,256]{1,0:T(8,128)(2,1)} %constant.5.clone.band_y) | copy-start | bytes 245764
  1.5 0.9 %copy-start.1 = (bf16[160,256]{1,0:T(8,128)(2,1)S(1)}, bf16[160,256]{1,0:T(8,128)(2,1)}, u32[]{:S(2)}) copy-start(bf16[160,256]{1,0:T(8,128)(2,1)} %constant.4.clone.band_x) | copy-start | bytes 245764
  2.4 0.7 %copy-start.2 = (s32[1,2]{1,0:T(1,128)S(1)}, s32[1,2]{1,0:T(1,128)}, u32[]{:S(2)}) copy-start(s32[1,2]{1,0:T(1,128)} %times.1) | copy-start | bytes 28
  3.1 0.7 %copy-start.3 = (s32[1,2]{1,0:T(1,128)S(1)}, s32[1,2]{1,0:T(1,128)}, u32[]{:S(2)}) copy-start(s32[1,2]{1,0:T(1,128)} %sources.1) | copy-start | bytes 28

commit v2 on v1

--- a/solution.py
+++ b/solution.py
@@ -13,27 +13,32 @@
 SIGMA_X = 0.5 * RADIUS
 SIGMA_Y = 0.375 * RADIUS
 ROWS = 16
-
-
-def band_parts(count, sigma):
+AHEAD = 3
+
+
+def fill_band(band, sigma):
+    count = band.shape[1] // 2
     taps = np.arange(-RADIUS, RADIUS + 1).astype(np.float64)
-    norm = np.exp(-taps * taps / (2.0 * sigma * sigma)).sum()
-    own = np.arange(count)
-    cells = np.concatenate([own, np.arange(-RADIUS, 0), np.arange(count, count + RADIUS)])
-    offset = (cells[:, None] - own[None, :]).astype(np.float64)
-    values = np.exp(-offset * offset / (2.0 * sigma * sigma)) / norm
-    values = np.where(np.abs(offset) <= RADIUS, values, 0.0).astype(np.float32)
+    norm = float(np.exp(-taps * taps / (2.0 * sigma * sigma)).sum())
+    row = lax.broadcasted_iota(jnp.int32, (count + 2 * RADIUS, count), 0)
+    own = lax.broadcasted_iota(jnp.int32, (count + 2 * RADIUS, count), 1)
+    left = jnp.logical_and(row >= count, row < count + RADIUS)
+    cell = jnp.where(row < count, row, jnp.where(left, row - count - RADIUS, row - RADIUS))
+    offset = cell - own
+    real = offset.astype(jnp.float32)
+    values = jnp.exp(-real * real / (2.0 * sigma * sigma)) / norm
+    values = jnp.where(jnp.abs(offset) <= RADIUS, values, 0.0)
     high = values.astype(jnp.bfloat16)
-    low = (values - high.astype(np.float32)).astype(jnp.bfloat16)
-    return np.concatenate([high, low], axis=1)
+    band[:, :count] = high
+    band[:, count:] = (values - high.astype(jnp.float32)).astype(jnp.bfloat16)
 
 
 def kernel(
     n, ng, nh, raw,
-    fwd, adj, times, sources, aperture, band_x, band_y,
+    fwd, adj, scalars_in,
     out,
-    fbuf, abuf, taper, wx, wy, sm, recv,
-    load_f, load_a, x_send, x_recv, gx_send, gx_recv, gy_send, gy_recv,
+    scalars, band_x, band_y, fbuf, abuf, taper, wx, wy, sm, recv,
+    small, load_f, load_a, x_send, x_recv, gx_send, gx_recv, gy_send, gy_recv,
 ):
     me = lax.axis_index("shot")
     g = lax.axis_index("gx")
@@ -56,7 +61,11 @@
             copy.start()
         return c
 
-    lax.fori_loop(0, levels, start_load, 0)
+    ahead = min(AHEAD, levels)
+    lax.fori_loop(0, 1, start_load, 0)
+    fetch = pltpu.make_async_copy(scalars_in, scalars, small)
+    fetch.start()
+    lax.fori_loop(1, ahead, start_load, 0)
 
     barrier = pltpu.get_barrier_semaphore()
     for d in range(1, n):
@@ -85,17 +94,21 @@
 
                 lax.fori_loop(0, levels, clear, 0)
 
+    fetch.wait()
     x_at = g * width_x + lax.broadcasted_iota(jnp.int32, (width_x, width_y), 0)
     y_at = h * width_y + lax.broadcasted_iota(jnp.int32, (width_x, width_y), 1)
-    dx = (x_at - sources[0, 0]).astype(jnp.float32)
-    dy = (y_at - sources[0, 1]).astype(jnp.float32)
-    taper[...] = (1.0 - jnp.exp(-(dx * dx + dy * dy) / (2.0 * MUTE * MUTE))) * aperture[
-        0, 0, 0
+    dx = (x_at - scalars[0, snaps]).astype(jnp.float32)
+    dy = (y_at - scalars[0, snaps + 1]).astype(jnp.float32)
+    taper[...] = (1.0 - jnp.exp(-(dx * dx + dy * dy) / (2.0 * MUTE * MUTE))) * scalars[
+        0, snaps + 2
     ].astype(jnp.float32)
+
+    fill_band(band_x, SIGMA_X)
+    fill_band(band_y, SIGMA_Y)
 
     weights = []
     for k in range(snaps):
-        step = times[0, k] - (times[0, k - 1] if k else 0)
+        step = scalars[0, k] - (scalars[0, k - 1] if k else 0)
         weights.append(step.astype(jnp.float32) * -0.125)
 
     def image(q):
@@ -191,6 +204,10 @@
         return lax.rem(q, here) < raw
 
     def make(q, c):
+        @pl.when(q + ahead < levels)
+        def _():
+            start_load(q + ahead, 0)
+
         for copy in load(q):
             copy.wait()
         image(q)
@@ -290,22 +307,35 @@
     lax.fori_loop(0, levels, done, 0)
 
 
+def store(cells, out, sems):
+    copies = [
+        pltpu.make_async_copy(cells.at[p], out.at[p], sems.at[p]) for p in range(cells.shape[0])
+    ]
+    for copy in copies:
+        copy.start()
+    for copy in copies:
+        copy.wait()
+
+
 def on_device(n, ng, nh, forward, adjoint, snap_times, sources, aperture):
     snaps, comps, levels, width_x, width_y = forward.shape[1:]
     here = levels // n
     peers = (n - 1) * here
     raw = here // 2
+    scalars = jnp.concatenate([snap_times, sources, aperture[:, :, 0]], axis=1)
     f32 = jnp.float32
     dma = pltpu.SemaphoreType.DMA
-    smem = pl.BlockSpec(memory_space=pltpu.SMEM)
     vmem = pl.BlockSpec(memory_space=pltpu.VMEM)
-    anywhere = pl.BlockSpec(memory_space=pl.ANY)
-    return pl.pallas_call(
+    hbm = pl.BlockSpec(memory_space=pltpu.HBM)
+    summed = pl.pallas_call(
         functools.partial(kernel, n, ng, nh, raw),
         out_shape=jax.ShapeDtypeStruct((3, here, width_x, width_y), f32),
-        in_specs=[anywhere, anywhere, smem, smem, smem, vmem, vmem],
+        in_specs=[hbm, hbm, pl.BlockSpec(memory_space=pl.ANY)],
         out_specs=vmem,
         scratch_shapes=[
+            pltpu.SMEM(scalars.shape, scalars.dtype),
+            pltpu.VMEM((width_x + 2 * RADIUS, 2 * width_x), jnp.bfloat16),
+            pltpu.VMEM((width_y + 2 * RADIUS, 2 * width_y), jnp.bfloat16),
             pltpu.VMEM((levels, snaps, comps, width_x, width_y), forward.dtype),
             pltpu.VMEM((levels, snaps, comps, width_x, width_y), adjoint.dtype),
             pltpu.VMEM((width_x, width_y), f32),
@@ -313,6 +343,7 @@
             pltpu.VMEM((levels, 3, width_y + 2 * RADIUS, width_x), f32),
             pltpu.VMEM((peers, 3, width_x, width_y), f32),
             pltpu.VMEM((peers, 3, width_x, width_y), f32),
+            dma,
             dma((levels,)),
             dma((levels,)),
             dma((peers,)),
@@ -331,9 +362,16 @@
             transcendentals=width_x * width_y,
         ),
     )(
-        forward, adjoint, snap_times, sources, aperture,
-        band_parts(width_x, SIGMA_X), band_parts(width_y, SIGMA_Y),
+        forward, adjoint, scalars
     )
+    return pl.pallas_call(
+        store,
+        out_shape=jax.ShapeDtypeStruct(summed.shape, summed.dtype),
+        in_specs=[vmem],
+        out_specs=hbm,
+        scratch_shapes=[dma((3,))],
+        compiler_params=pltpu.CompilerParams(vmem_limit_bytes=4 * 1024 * 1024),
+    )(summed)
 
 
 def solution(mesh):

time: 46.9 us -> 43.7 us (0.932)
  local copies, waits for them, and re-layouts: 4.22 us -> 0 us
  other arithmetic: 0 us -> 0.75 us
    unnamed x9 -> x0, local copies, waits for them, and re-layouts: 4.22 us -> none
    pallas_call x0 -> x1, Pallas kernels: none -> 1.17 us  [on_device(): pl.pallas_call(store, out_shape=jax.ShapeDtypeStruct(summed.shape, summed...]
    pallas_call x1, Pallas kernels: 41.8 us -> 41 us  [on_device(): pl.pallas_call(functools.partial(kernel, n, ng, nh, raw), out_shape=jax.S...]
    concatenate x0 -> x1, other arithmetic: none -> 0.75 us  [on_device(): scalars = jnp.concatenate([snap_times, sources, aperture[:, :, 0]], axis=1)]
where the time goes in v2:
time: 43.7 us; the launch traced here: 43.5 us
  Pallas kernels  42.1 us (96%)
  other arithmetic  0.75 us (2%)
  between operations  0.66 us (2%)
    pallas_call x1, Pallas kernels, on_device(): pl.pallas_call(functools.partial(kernel, n, ng, nh, raw), out_shape=jax.S...  41 us
    pallas_call x1, Pallas kernels, on_device(): pl.pallas_call(store, out_shape=jax.ShapeDtypeStruct(summed.shape, summed...  1.17 us

profile of v2, /device:TPU:0, one launch (start us, length us, event | category | flops | bytes accessed | tf_op | source)
XLA Modules:
  0.0 43.5 jit_solution(14768085290354965305)
XLA Ops:
  0.7 0.7 %pad_add_fusion.scalars_in = s32[1,5]{1,0:T(1,128)S(1)} fusion(s32[1,1]{1,0:T(1,128)} %bitcast.1, s32[1,2]{1,0:T(1,128)} %param.8, s32[1,2]{1,0:T(1,128)} %param.7), kind=kLoop, calls=%fused_computation | loop fusion | flops 10 | bytes 40 | tf_op jit(solution)/shard_map/concatenate | solution.py:325
  1.4 41.0 %shard_map.55.cells = f32[3,8,128,128]{3,2,1,0:T(8,128)S(1)} custom-call(bf16[1,2,9,16,128,128]{5,4,3,2,1,0:T(8,128)(2,1)} %fwd.1, bf16[1,2,9,16,128,128]{5,4,3,2,1,0:T(8,128)(2,1)} %adj.1, s32[1,5]{1,0:T(1,128)S(1)} %pad_add_fusion.scalars_in), custom_call_target="tpu_custom_call" | custom-call | flops 37748736 | bytes 20447232 | tf_op jit(solution)/shard_map/pallas_call | solution.py:330
  42.4 1.2 %shard_map.56 = f32[3,8,128,128]{3,2,1,0:T(8,128)} custom-call(f32[3,8,128,128]{3,2,1,0:T(8,128)S(1)} %shard_map.55.cells), custom_call_target="tpu_custom_call" | custom-call | tf_op jit(solution)/shard_map/pallas_call | solution.py:367

commit v3 on v2

--- a/solution.py
+++ b/solution.py
@@ -49,6 +49,21 @@
     here = levels // n
     peers = (n - 1) * here
 
+    barrier = pltpu.get_barrier_semaphore()
+    for d in range(1, n):
+        pl.semaphore_signal(barrier, inc=1, device_id={"shot": lax.rem(me + d, n)})
+    greeted = jnp.int32(n - 1)
+    for axis, at, count in (("gx", g, ng), ("gy", h, nh)):
+        @pl.when(at > 0)
+        def _():
+            pl.semaphore_signal(barrier, inc=1, device_id={axis: at - 1})
+
+        @pl.when(at < count - 1)
+        def _():
+            pl.semaphore_signal(barrier, inc=1, device_id={axis: at + 1})
+
+        greeted = greeted + (at > 0).astype(jnp.int32) + (at < count - 1).astype(jnp.int32)
+
     def load(q):
         level = lax.rem(me + q // here + 1, n) * here + lax.rem(q, here)
         return (
@@ -66,33 +81,6 @@
     fetch = pltpu.make_async_copy(scalars_in, scalars, small)
     fetch.start()
     lax.fori_loop(1, ahead, start_load, 0)
-
-    barrier = pltpu.get_barrier_semaphore()
-    for d in range(1, n):
-        pl.semaphore_signal(barrier, inc=1, device_id={"shot": lax.rem(me + d, n)})
-    greeted = jnp.int32(n - 1)
-    for axis, at, count in (("gx", g, ng), ("gy", h, nh)):
-        @pl.when(at > 0)
-        def _():
-            pl.semaphore_signal(barrier, inc=1, device_id={axis: at - 1})
-
-        @pl.when(at < count - 1)
-        def _():
-            pl.semaphore_signal(barrier, inc=1, device_id={axis: at + 1})
-
-        greeted = greeted + (at > 0).astype(jnp.int32) + (at < count - 1).astype(jnp.int32)
-
-    for buf, at, count, width in ((wx, g, ng, width_x), (wy, h, nh, width_y)):
-        for there, start in ((at > 0, width), (at < count - 1, width + RADIUS)):
-            @pl.when(jnp.logical_not(there))
-            def _():
-                def clear(q, c):
-                    buf[q, :, start:start + RADIUS, :] = jnp.zeros(
-                        (3, RADIUS, buf.shape[3]), jnp.float32
-                    )
-                    return c
-
-                lax.fori_loop(0, levels, clear, 0)
 
     fetch.wait()
     x_at = g * width_x + lax.broadcasted_iota(jnp.int32, (width_x, width_y), 0)
@@ -102,9 +90,6 @@
     taper[...] = (1.0 - jnp.exp(-(dx * dx + dy * dy) / (2.0 * MUTE * MUTE))) * scalars[
         0, snaps + 2
     ].astype(jnp.float32)
-
-    fill_band(band_x, SIGMA_X)
-    fill_band(band_y, SIGMA_Y)
 
     weights = []
     for k in range(snaps):
@@ -228,6 +213,21 @@
 
     lax.fori_loop(0, levels, make, 0)
 
+    for buf, at, count, width in ((wx, g, ng, width_x), (wy, h, nh, width_y)):
+        for there, start in ((at > 0, width), (at < count - 1, width + RADIUS)):
+            @pl.when(jnp.logical_not(there))
+            def _():
+                def clear(q, c):
+                    buf[q, :, start:start + RADIUS, :] = jnp.zeros(
+                        (3, RADIUS, buf.shape[3]), jnp.float32
+                    )
+                    return c
+
+                lax.fori_loop(0, levels, clear, 0)
+
+    fill_band(band_x, SIGMA_X)
+    fill_band(band_y, SIGMA_Y)
+
     def first_x(q, c):
         @pl.when(jnp.logical_not(is_raw(q)))
         def _():
@@ -261,7 +261,7 @@
     def sum_raw(i, c):
         for d in range(n - 1):
             q = d * here + i
-            x_copy(wx.at[q, :, pl.ds(0, width_x), :], q).wait_recv()
+            x_copy(wx.at[q, :, pl.ds(0, width_x), :], q).wait()
         for p in range(3):
             total = wx[peers + i, p, 0:width_x, :]
             for d in range(n - 1):
@@ -279,10 +279,20 @@
     lax.fori_loop(0, raw, raw_x, 0)
     lax.fori_loop(0, raw, to_out, 0)
 
+    def done(q, c):
+        @pl.when(jnp.logical_or(q >= peers, jnp.logical_not(is_raw(q))))
+        def _():
+            halo_sent("gx", q)
+            halo_sent("gy", q)
+
+        return c
+
+    lax.fori_loop(0, levels, done, 0)
+
     def add(i, c):
         for d in range(n - 1):
             q = d * here + i
-            x_copy(sm.at[q], q).wait_recv()
+            x_copy(sm.at[q], q).wait()
         for p in range(3):
             total = out[p, i]
             for d in range(n - 1):
@@ -291,20 +301,6 @@
         return c
 
     lax.fori_loop(raw, here, add, 0)
-
-    def done(q, c):
-        @pl.when(q < peers)
-        def _():
-            x_copy(sm.at[q], q).wait_send()
-
-        @pl.when(jnp.logical_or(q >= peers, jnp.logical_not(is_raw(q))))
-        def _():
-            halo_sent("gx", q)
-            halo_sent("gy", q)
-
-        return c
-
-    lax.fori_loop(0, levels, done, 0)
 
 
 def store(cells, out, sems):

time: 43.7 us -> 43.5 us (level)
  no operation moved by 1% of the time
where the time goes in v3:
time: 43.5 us; the launch traced here: 43.3 us
  Pallas kernels  41.9 us (96%)
  other arithmetic  0.75 us (2%)
  between operations  0.66 us (2%)
    pallas_call x1, Pallas kernels, on_device(): pl.pallas_call(functools.partial(kernel, n, ng, nh, raw), out_shape=jax.S...  40.7 us
    pallas_call x1, Pallas kernels, on_device(): pl.pallas_call(store, out_shape=jax.ShapeDtypeStruct(summed.shape, summed...  1.17 us

profile of v3, /device:TPU:0, one launch (start us, length us, event | category | flops | bytes accessed | tf_op | source)
XLA Modules:
  0.0 43.3 jit_solution(12599967700635087331)
XLA Ops:
  0.7 0.7 %pad_add_fusion.scalars_in = s32[1,5]{1,0:T(1,128)S(1)} fusion(s32[1,1]{1,0:T(1,128)} %bitcast.1, s32[1,2]{1,0:T(1,128)} %param.8, s32[1,2]{1,0:T(1,128)} %param.7), kind=kLoop, calls=%fused_computation | loop fusion | flops 10 | bytes 40 | tf_op jit(solution)/shard_map/concatenate | solution.py:321
  1.4 40.7 %shard_map.55.cells = f32[3,8,128,128]{3,2,1,0:T(8,128)S(1)} custom-call(bf16[1,2,9,16,128,128]{5,4,3,2,1,0:T(8,128)(2,1)} %fwd.1, bf16[1,2,9,16,128,128]{5,4,3,2,1,0:T(8,128)(2,1)} %adj.1, s32[1,5]{1,0:T(1,128)S(1)} %pad_add_fusion.scalars_in), custom_call_target="tpu_custom_call" | custom-call | flops 37748736 | bytes 20447232 | tf_op jit(solution)/shard_map/pallas_call | solution.py:326
  42.1 1.2 %shard_map.56 = f32[3,8,128,128]{3,2,1,0:T(8,128)} custom-call(f32[3,8,128,128]{3,2,1,0:T(8,128)S(1)} %shard_map.55.cells), custom_call_target="tpu_custom_call" | custom-call | tf_op jit(solution)/shard_map/pallas_call | solution.py:363
